TPU v7x, 32 devices: a whole 2x2x4 slice. The times are simulated.
32 devices in a mesh: outer: 8 (over z, y), inner: 4 (over x, core).
Axes of the slice: x: 2, y: 2, z: 4, core: 2. Of those that a mesh axis runs over, the one named last changes fastest.
Arguments:
- image_embeds: bfloat16 [16384, 512], P(('outer', 'inner')), may hold values from -0.17766058 to 0.17766058
- text_embeds: bfloat16 [16384, 512], P(('outer', 'inner')), may hold values from -0.17766058 to 0.17766058
- image_lse: float32 [16384], P(('outer', 'inner')), as said below
- text_lse: float32 [16384], P(('outer', 'inner')), as said below
- logit_scale: float32 [], replicated, may hold values from 90 to 100, as said below
Outputs:
- image_grad: float32 [16384, 512], P(('outer', 'inner'))
- text_grad: float32 [16384, 512], P(('outer', 'inner'))
Inputs may be any that keep to these rules, and one draw needn't show every extreme that they name: logit_scale is one positive number. `image_lse`: saved by the forward pass: for image row i, the log of the sum of exp(score_ij) over the text rows j that the window pairs with it. `text_lse`: saved by the forward pass: for text row j, the log of the sum of exp(score_ij) over the image rows i that the window pairs with it.
All inputs are finite; a program needn't handle non-finite values.
Results may differ from a plain program's by a relative error of at most 0.0013.
Values may be sent and summed in bfloat16 or wider, within the bound.
A program may use at most 64 MiB of HBM per device.

v0:
```python
import jax
import jax.numpy as jnp
from jax import lax
from jax.sharding import PartitionSpec as P


def shifted(value, axis, steps):
    count = lax.axis_size(axis)
    pairs = [(source, (source + steps) % count) for source in range(count)]
    return lax.ppermute(value, axis, pairs)


def split_exact(values):
    upper_part = lax.optimization_barrier(values.astype(jnp.bfloat16))
    remainder = values - upper_part.astype(jnp.float32)
    middle = lax.optimization_barrier(remainder.astype(jnp.bfloat16))
    lower_part = (remainder - middle.astype(jnp.float32)).astype(jnp.bfloat16)
    return jnp.stack([upper_part, middle, lower_part])


def join_exact(pieces):
    widened = pieces.astype(jnp.float32)
    return widened[0] + (widened[1] + widened[2])


def tile_weights(images, image_stat, text_rows, text_stat, factor):
    scores = factor * lax.dot_general(
        images, text_rows, (((1,), (1,)), ((), ())), preferred_element_type=jnp.float32
    )
    return (jnp.exp(scores - image_stat[:, None]) + jnp.exp(scores - text_stat[None, :])).astype(
        jnp.bfloat16
    )


def image_side(weights, text_rows):
    return jnp.dot(weights, text_rows, preferred_element_type=jnp.float32)


def text_side(weights, images):
    return lax.dot_general(
        weights, images, (((0,), (0,)), ((), ())), preferred_element_type=jnp.float32
    )


def local(image_embeds, text_embeds, image_lse, text_lse, logit_scale):
    text_pieces = split_exact(text_lse)
    own_weights = tile_weights(image_embeds, image_lse, text_embeds, text_lse, logit_scale)
    image_total = image_side(own_weights, text_embeds)
    own_text = text_side(own_weights, image_embeds)
    near_text, near_pieces = shifted((text_embeds, text_pieces), "inner", 1)
    far_text, far_pieces, both_text, both_pieces = shifted(
        (text_embeds, text_pieces, near_text, near_pieces), "outer", 1
    )
    near_weights = tile_weights(
        image_embeds, image_lse, near_text, join_exact(near_pieces), logit_scale
    )
    far_weights = tile_weights(
        image_embeds, image_lse, far_text, join_exact(far_pieces), logit_scale
    )
    both_weights = tile_weights(
        image_embeds, image_lse, both_text, join_exact(both_pieces), logit_scale
    )
    image_total = (
        image_total
        + image_side(near_weights, near_text)
        + image_side(far_weights, far_text)
        + image_side(both_weights, both_text)
    )
    back_far, back_both = shifted(
        (text_side(far_weights, image_embeds), text_side(both_weights, image_embeds)), "outer", -1
    )
    second_sum = text_side(near_weights, image_embeds) + back_both
    returned = shifted(second_sum, "inner", -1)
    text_total = own_text + back_far + returned
    image_grad = logit_scale * (image_total - 2.0 * text_embeds.astype(jnp.float32))
    text_grad = logit_scale * (text_total - 2.0 * image_embeds.astype(jnp.float32))
    return (image_grad, text_grad)


def solution(mesh):
    return jax.shard_map(
        local,
        mesh=mesh,
        in_specs=(
            P(("outer", "inner"), None),
            P(("outer", "inner"), None),
            P(("outer", "inner")),
            P(("outer", "inner")),
            P(),
        ),
        out_specs=(P(("outer", "inner"), None), P(("outer", "inner"), None)),
        check_vma=False,
    )
```

profile of v0, /device:TPU:0, one launch (start us, length us, event | category | flops | bytes accessed | tf_op | source)
XLA Modules:
  0.0 87.0 jit_solution(10945880082717340611)
XLA Ops:
  0.6 0.5 collective-permute-start
  1.1 0.7 convert_element_type.43
  1.8 0.7 copy-done.2
  2.5 7.6 %collective-permute-done = bf16[512,512]{1,0:T(8,128)(2,1)S(1)} collective-permute-done((bf16[512,512]{1,0:T(8,128)(2,1)}, bf16[512,512]{1,0:T(8,128)(2,1)S(1)}, u32[]{:S(2)}, u32[]{:S(2)}) %collective-permute-start) | collective-permute-done | bytes 524320 | tf_op jit(solution)/shard_map/ppermute | solution.py:10
  10.1 2.3 %collective-permute-start.4 = (bf16[512,512]{1,0:T(8,128)(2,1)S(1)}, bf16[512,512]{1,0:T(8,128)(2,1)S(1)}, u32[]{:S(2)}, u32[]{:S(2)}) collective-permute-start(bf16[512,512]{1,0:T(8,128)(2,1)S(1)} %collective-permute-done), channel_id=1, source_target_pairs={{0,4},{4,8},{8,12},{12,16},{16,20},{20,24},{24,28},{28,0},{1,5},{5... | collective-permute-start | bytes 1572872 | tf_op jit(solution)/shard_map/ppermute | solution.py:10
  12.5 1.6 %collective-permute-start.2 = (bf16[512,512]{1,0:T(8,128)(2,1)}, bf16[512,512]{1,0:T(8,128)(2,1)S(1)}, u32[]{:S(2)}, u32[]{:S(2)}) collective-permute-start(bf16[512,512]{1,0:T(8,128)(2,1)} %param.6), channel_id=1, source_target_pairs={{0,4},{4,8},{8,12},{12,16},{16,20},{20,24},{24,28},{28,0},{1,5},{5... | collective-permute-start | bytes 1572872 | tf_op jit(solution)/shard_map/ppermute | solution.py:10
  14.1 1.5 %collective-permute-start.3 = (bf16[3,512]{1,0:T(4,128)(2,1)S(1)}, bf16[3,512]{1,0:T(4,128)(2,1)S(1)}, u32[]{:S(2)}, u32[]{:S(2)}) collective-permute-start(bf16[3,512]{1,0:T(4,128)(2,1)S(1)} %pad_maximum_fusion), channel_id=1, source_target_pairs={{0,4},{4,8},{8,12},{12,16},{16,20},{20,24},{24,28},{28,0},{1,5},{5... | collective-permute-start | bytes 9224 | tf_op jit(solution)/shard_map/ppermute | solution.py:10
  16.3 1.6 %collective-permute-start.5 = (bf16[3,512]{1,0:T(4,128)(2,1)S(1)}, bf16[3,512]{1,0:T(4,128)(2,1)S(1)}, u32[]{:S(2)}, u32[]{:S(2)}) collective-permute-start(bf16[3,512]{1,0:T(4,128)(2,1)S(1)} %collective-permute-done.1), channel_id=1, source_target_pairs={{0,4},{4,8},{8,12},{12,16},{16,20},{20,24},{24,28},{28,0},{1,5},{5... | collective-permute-start | bytes 9224 | tf_op jit(solution)/shard_map/ppermute | solution.py:10
  17.9 1.8 %add_convert_fusion.3 = bf16[512,512]{1,0:T(8,128)(2,1)S(1)} fusion(bf16[512,512]{1,0:T(8,128)(2,1)} %param.5, bf16[512,512]{1,0:T(8,128)(2,1)} %param.6, f32[512]{0:T(512)S(1)} %copy-done.2, f32[512]{0:T(512)S(1)} %copy-done.3, f32[]{:T(128)S(6)} %copy.7), kind=kOutput, calls=%fused_computation.17 | convolution fusion | flops 269746176 | bytes 1576964 | tf_op jit(solution)/shard_map/dot_general | solution.py:27
  19.7 18.5 %collective-permute-done.5 = bf16[3,512]{1,0:T(4,128)(2,1)S(1)} collective-permute-done((bf16[3,512]{1,0:T(4,128)(2,1)S(1)}, bf16[3,512]{1,0:T(4,128)(2,1)S(1)}, u32[]{:S(2)}, u32[]{:S(2)}) %collective-permute-start.5) | collective-permute-done | bytes 3104 | tf_op jit(solution)/shard_map/ppermute | solution.py:10
  38.3 0.6 add_convert_fusion
  38.9 0.5 fusion.11
  39.4 1.8 %collective-permute-start.7 = (f32[512,512]{1,0:T(8,128)S(1)}, f32[512,512]{1,0:T(8,128)S(1)}, u32[]{:S(2)}, u32[]{:S(2)}) collective-permute-start(f32[512,512]{1,0:T(8,128)S(1)} %fusion.11), channel_id=1, source_target_pairs={{0,28},{4,0},{8,4},{12,8},{16,12},{20,16},{24,20},{28,24},{1,29},{... | collective-permute-start | bytes 3145736 | tf_op jit(solution)/shard_map/ppermute | solution.py:10
  41.2 0.6 add_convert_fusion.1
  41.9 0.5 fusion.10
  42.3 1.5 %collective-permute-start.6 = (f32[512,512]{1,0:T(8,128)S(1)}, f32[512,512]{1,0:T(8,128)S(1)}, u32[]{:S(2)}, u32[]{:S(2)}) collective-permute-start(f32[512,512]{1,0:T(8,128)S(1)} %fusion.10), channel_id=1, source_target_pairs={{0,28},{4,0},{8,4},{12,8},{16,12},{20,16},{24,20},{28,24},{1,29},{... | collective-permute-start | bytes 3145736 | tf_op jit(solution)/shard_map/ppermute | solution.py:10
  43.8 0.6 add_convert_fusion.2
  44.4 21.1 %collective-permute-done.7 = f32[512,512]{1,0:T(8,128)S(1)} collective-permute-done((f32[512,512]{1,0:T(8,128)S(1)}, f32[512,512]{1,0:T(8,128)S(1)}, u32[]{:S(2)}, u32[]{:S(2)}) %collective-permute-start.7) | collective-permute-done | bytes 1048608 | tf_op jit(solution)/shard_map/ppermute | solution.py:10
  65.5 0.5 convolution_add_fusion
  66.1 0.4 fusion.9
  66.5 0.4 convolution_add_fusion.4
  67.4 1.4 %fusion.4 = f32[512,512]{1,0:T(8,128)} fusion(f32[512,512]{1,0:T(8,128)S(1)} %convolution_add_fusion.3, bf16[512,512]{1,0:T(8,128)(2,1)S(1)} %add_convert_fusion, bf16[512,512]{1,0:T(8,128)(2,1)S(1)} %collective-permute-done.4, bf16[512,512]{1,0:T(8,128)(2,1)S(1)} %copy-done.1, f32[]{:T(128)S(6)} %copy.7), kind=kOutput, calls=%fused_computation.7 | convolution fusion | flops 269746176 | bytes 3670020 | tf_op jit(solution)/shard_map/dot_general | solution.py:36
  68.8 16.7 %collective-permute-done.6 = f32[512,512]{1,0:T(8,128)S(1)} collective-permute-done((f32[512,512]{1,0:T(8,128)S(1)}, f32[512,512]{1,0:T(8,128)S(1)}, u32[]{:S(2)}, u32[]{:S(2)}) %collective-permute-start.6) | collective-permute-done | bytes 1048608 | tf_op jit(solution)/shard_map/ppermute | solution.py:10
  85.6 1.5 %fusion.2 = f32[512,512]{1,0:T(8,128)} fusion(f32[512,512]{1,0:T(8,128)S(1)} %collective-permute-done.8, f32[512,512]{1,0:T(8,128)S(1)} %collective-permute-done.6, bf16[512,512]{1,0:T(8,128)(2,1)S(1)} %add_convert_fusion.3, bf16[512,512]{1,0:T(8,128)(2,1)S(1)} %copy-done, f32[]{:T(128)S(6)} %copy.7), kind=kOutput, calls=%fused_computation.4 | convolution fusion | flops 270008320 | bytes 4194308 | tf_op jit(solution)/shard_map/dot_general | solution.py:40
  (27 shorter events, 0.7 us)
Async XLA Ops:
  0.6 9.5 %collective-permute-start = (bf16[512,512]{1,0:T(8,128)(2,1)}, bf16[512,512]{1,0:T(8,128)(2,1)S(1)}, u32[]{:S(2)}, u32[]{:S(2)}) collective-permute-start(bf16[512,512]{1,0:T(8,128)(2,1)} %param.6), channel_id=1, source_target_pairs={{0,1},{1,2},{2,3},{3,0},{4,5},{5,6},{6,7},{7,4},{8,9},{9,10},{10,1... | collective-permute-start | bytes 1572872 | tf_op jit(solution)/shard_map/ppermute | solution.py:10
  1.8 0.7 copy-start.2
  2.5 15.4 %copy-start.3 = (f32[512]{0:T(512)S(1)}, f32[512]{0:T(512)}, u32[]{:S(2)}) copy-start(f32[512]{0:T(512)} %param.7) | copy-start | bytes 6148
  10.1 28.1 %collective-permute-start.4 = (bf16[512,512]{1,0:T(8,128)(2,1)S(1)}, bf16[512,512]{1,0:T(8,128)(2,1)S(1)}, u32[]{:S(2)}, u32[]{:S(2)}) collective-permute-start(bf16[512,512]{1,0:T(8,128)(2,1)S(1)} %collective-permute-done), channel_id=1, source_target_pairs={{0,4},{4,8},{8,12},{12,16},{16,20},{20,24},{24,28},{28,0},{1,5},{5... | collective-permute-start | bytes 1572872 | tf_op jit(solution)/shard_map/ppermute | solution.py:10
  12.5 3.8 %collective-permute-start.1 = (bf16[3,512]{1,0:T(4,128)(2,1)S(1)}, bf16[3,512]{1,0:T(4,128)(2,1)S(1)}, u32[]{:S(2)}, u32[]{:S(2)}) collective-permute-start(bf16[3,512]{1,0:T(4,128)(2,1)S(1)} %pad_maximum_fusion), channel_id=1, source_target_pairs={{0,1},{1,2},{2,3},{3,0},{4,5},{5,6},{6,7},{7,4},{8,9},{9,10},{10,1... | collective-permute-start | bytes 9224 | tf_op jit(solution)/shard_map/ppermute | solution.py:10
  12.5 28.7 %collective-permute-start.2 = (bf16[512,512]{1,0:T(8,128)(2,1)}, bf16[512,512]{1,0:T(8,128)(2,1)S(1)}, u32[]{:S(2)}, u32[]{:S(2)}) collective-permute-start(bf16[512,512]{1,0:T(8,128)(2,1)} %param.6), channel_id=1, source_target_pairs={{0,4},{4,8},{8,12},{12,16},{16,20},{20,24},{24,28},{28,0},{1,5},{5... | collective-permute-start | bytes 1572872 | tf_op jit(solution)/shard_map/ppermute | solution.py:10
  14.1 27.1 %collective-permute-start.3 = (bf16[3,512]{1,0:T(4,128)(2,1)S(1)}, bf16[3,512]{1,0:T(4,128)(2,1)S(1)}, u32[]{:S(2)}, u32[]{:S(2)}) collective-permute-start(bf16[3,512]{1,0:T(4,128)(2,1)S(1)} %pad_maximum_fusion), channel_id=1, source_target_pairs={{0,4},{4,8},{8,12},{12,16},{16,20},{20,24},{24,28},{28,0},{1,5},{5... | collective-permute-start | bytes 9224 | tf_op jit(solution)/shard_map/ppermute | solution.py:10
  16.3 22.0 %copy-start = (bf16[512,512]{1,0:T(8,128)(2,1)S(1)}, bf16[512,512]{1,0:T(8,128)(2,1)}, u32[]{:S(2)}) copy-start(bf16[512,512]{1,0:T(8,128)(2,1)} %param.5) | copy-start | bytes 1572868
  16.3 21.9 %collective-permute-start.5 = (bf16[3,512]{1,0:T(4,128)(2,1)S(1)}, bf16[3,512]{1,0:T(4,128)(2,1)S(1)}, u32[]{:S(2)}, u32[]{:S(2)}) collective-permute-start(bf16[3,512]{1,0:T(4,128)(2,1)S(1)} %collective-permute-done.1), channel_id=1, source_target_pairs={{0,4},{4,8},{8,12},{12,16},{16,20},{20,24},{24,28},{28,0},{1,5},{5... | collective-permute-start | bytes 9224 | tf_op jit(solution)/shard_map/ppermute | solution.py:10
  39.4 26.1 %collective-permute-start.7 = (f32[512,512]{1,0:T(8,128)S(1)}, f32[512,512]{1,0:T(8,128)S(1)}, u32[]{:S(2)}, u32[]{:S(2)}) collective-permute-start(f32[512,512]{1,0:T(8,128)S(1)} %fusion.11), channel_id=1, source_target_pairs={{0,28},{4,0},{8,4},{12,8},{16,12},{20,16},{24,20},{28,24},{1,29},{... | collective-permute-start | bytes 3145736 | tf_op jit(solution)/shard_map/ppermute | solution.py:10
  42.3 43.2 %collective-permute-start.6 = (f32[512,512]{1,0:T(8,128)S(1)}, f32[512,512]{1,0:T(8,128)S(1)}, u32[]{:S(2)}, u32[]{:S(2)}) collective-permute-start(f32[512,512]{1,0:T(8,128)S(1)} %fusion.10), channel_id=1, source_target_pairs={{0,28},{4,0},{8,4},{12,8},{16,12},{20,16},{24,20},{28,24},{1,29},{... | collective-permute-start | bytes 3145736 | tf_op jit(solution)/shard_map/ppermute | solution.py:10
  44.4 21.6 %copy-start.1 = (bf16[512,512]{1,0:T(8,128)(2,1)S(1)}, bf16[512,512]{1,0:T(8,128)(2,1)}, u32[]{:S(2)}) copy-start(bf16[512,512]{1,0:T(8,128)(2,1)} %param.6) | copy-start | bytes 1572868
  66.0 19.6 %collective-permute-start.8 = (f32[512,512]{1,0:T(8,128)S(1)}, f32[512,512]{1,0:T(8,128)S(1)}, u32[]{:S(2)}, u32[]{:S(2)}) collective-permute-start(f32[512,512]{1,0:T(8,128)S(1)} %convolution_add_fusion), channel_id=1, source_target_pairs={{0,3},{1,0},{2,1},{3,2},{4,7},{5,4},{6,5},{7,6},{8,11},{9,8},{10,9... | collective-permute-start | bytes 3145736 | tf_op jit(solution)/shard_map/ppermute | solution.py:10
where the time goes:
time: 87.2 us; the launch traced here: 87 us
  waiting for transfers between devices  63.9 us (73%)
  starting transfers between devices  10.9 us (12%)
  matrix products  9.32 us (11%)
  between operations  1.46 us (2%)
    ppermute x9, waiting for transfers between devices, shifted(): return lax.ppermute(value, axis, pairs)  63.9 us
    ppermute x9, starting transfers between devices, shifted(): return lax.ppermute(value, axis, pairs)  10.9 us
    dot_general x4, matrix products, tile_weights(): lax.dot_general(images, text_rows, (((1,), (1,)), ((), ())), preferred_el...  3.74 us
    dot_general x4, matrix products, text_side(): lax.dot_general(weights, images, (((0,), (0,)), ((), ())), preferred_elem...  2.86 us
    dot_general x4, matrix products, image_side(): return jnp.dot(weights, text_rows, preferred_element_type=jnp.float32)  2.72 us
  transfers between devices with their start and end apart: 9, of which 4 were waited for; matrix products, arithmetic and copies ran while one was open for 10% of the time, Pallas kernels for 0%

commit v1 on v0

v1 whole, which is shorter than its diff:
```python
import functools
import math

import jax
import jax.numpy as jnp
from jax import lax
from jax.experimental import pallas as pl
from jax.experimental.pallas import tpu as pltpu
from jax.sharding import PartitionSpec as P

MESH = pl.DeviceIdType.MESH
LOG2E = math.log2(math.e)
LANES = 128
NEAR, FAR, BOTH = 0, 1, 2
NT = (((1,), (1,)), ((), ()))


def kernel(
    piece,
    scale_ref,
    images_ref,
    texts_ref,
    image_lse_ref,
    text_lse_ref,
    image_grad_ref,
    text_grad_ref,
    held,
    stat,
    column,
    got,
    got_stat,
    total,
    load_sem,
    send_sem,
    recv_sem,
    stat_send_sem,
    stat_recv_sem,
    out_sem,
):
    rows, width = images_ref.shape
    pieces = rows // piece
    outer, inner = lax.axis_index("outer"), lax.axis_index("inner")
    n_outer, n_inner = lax.axis_size("outer"), lax.axis_size("inner")
    scale = scale_ref[0, 0]
    factor = scale * LOG2E

    loads = [
        pltpu.make_async_copy(source, target, load_sem.at[index])
        for index, (source, target) in enumerate(
            [
                (texts_ref, held.at[0]),
                (images_ref, held.at[1]),
                (text_lse_ref, stat.at[0]),
                (image_lse_ref, stat.at[1]),
            ]
        )
    ]
    for load in loads:
        load.start()

    barrier = pltpu.get_barrier_semaphore()
    for step in (1, -1):
        pl.semaphore_signal(
            barrier, inc=1, device_id={"outer": (outer + step + n_outer) % n_outer},
            device_id_type=MESH,
        )
        pl.semaphore_signal(
            barrier, inc=1, device_id={"inner": (inner + step + n_inner) % n_inner},
            device_id_type=MESH,
        )
    pl.semaphore_wait(barrier, 4)
    for load in loads:
        load.wait()

    side_a = 1 - inner % 2
    side_b = inner % 2

    def target(kind, side):
        step = 1 - 2 * side
        if kind == FAR:
            return {"outer": (outer + step + n_outer) % n_outer}
        return {"inner": (inner + step + n_inner) % n_inner}

    def span(c):
        return pl.ds(pl.multiple_of(c * piece, piece), piece)

    def block_copy(kind, side, c):
        source = got.at[FAR, side, span(c)] if kind == BOTH else held.at[side, span(c)]
        return pltpu.make_async_remote_copy(
            src_ref=source,
            dst_ref=got.at[kind, side, span(c)],
            send_sem=send_sem.at[kind, side, c],
            recv_sem=recv_sem.at[kind, side, c],
            device_id=target(kind, side),
            device_id_type=MESH,
        )

    def stat_copy(kind, side):
        source = got_stat.at[FAR, side] if kind == BOTH else stat.at[side]
        return pltpu.make_async_remote_copy(
            src_ref=source,
            dst_ref=got_stat.at[kind, side],
            send_sem=stat_send_sem.at[kind, side],
            recv_sem=stat_recv_sem.at[kind, side],
            device_id=target(kind, side),
            device_id_type=MESH,
        )

    def for_pieces(body):
        def step(c, carry):
            body(c)
            return carry

        lax.fori_loop(0, pieces, step, 0)

    for side in (side_a, side_b):
        for kind in (FAR, NEAR):
            stat_copy(kind, side).start()

    def send_first(c):
        block_copy(FAR, side_a, c).start()
        block_copy(NEAR, side_a, c).start()

    def send_near(c):
        block_copy(NEAR, side_b, c).start()

    def send_far(c):
        block_copy(FAR, side_b, c).start()

    for_pieces(send_first)
    for_pieces(send_near)
    for_pieces(send_far)

    for side in (0, 1):
        column[side] = jnp.broadcast_to(stat[side] * LOG2E, (LANES, rows)).T

    def contribution(side, start, size, block, row):
        scores = factor * lax.dot_general(
            held[1 - side, pl.ds(start, size), :], block, NT,
            preferred_element_type=jnp.float32,
        )
        wide = jnp.concatenate(
            [column[1 - side, pl.ds(start, size), :]] * (block.shape[0] // LANES), axis=1
        )
        weights = (jnp.exp2(scores - wide) + jnp.exp2(scores - row)).astype(jnp.bfloat16)
        return jnp.dot(weights, block, preferred_element_type=jnp.float32)

    band = 256

    def add_piece(kind, side, c):
        block = got[kind, side, span(c), :]
        row = got_stat[kind, side, :, span(c)] * LOG2E
        for start in range(0, rows, band):
            total[side, pl.ds(start, band), :] += contribution(side, start, band, block, row)

    for side in (0, 1):
        block = held[side]
        row = stat[side] * LOG2E
        for start in range(0, rows, band):
            total[side, pl.ds(start, band), :] = contribution(side, start, band, block, row)

    def receive(kind, side, c):
        block_copy(kind, side, c).wait_recv()

    stat_copy(NEAR, side_a).wait_recv()

    def near_a(c):
        receive(NEAR, side_a, c)
        add_piece(NEAR, side_a, c)

    for_pieces(near_a)

    for side in (side_a, side_b):
        stat_copy(FAR, side).wait_recv()
        stat_copy(BOTH, side).start()
    stat_copy(NEAR, side_b).wait_recv()

    def early(c):
        receive(FAR, side_a, c)
        block_copy(BOTH, side_a, c).start()
        add_piece(FAR, side_a, c)
        receive(NEAR, side_b, c)
        add_piece(NEAR, side_b, c)

    for_pieces(early)

    for side in (side_a, side_b):
        stat_copy(BOTH, side).wait_recv()

    def late(c):
        receive(FAR, side_b, c)
        block_copy(BOTH, side_b, c).start()
        add_piece(FAR, side_b, c)
        receive(BOTH, side_b, c)
        add_piece(BOTH, side_b, c)

        @pl.when(c > 0)
        def _():
            receive(BOTH, side_a, c - 1)
            add_piece(BOTH, side_a, c - 1)

    for_pieces(late)

    def out_copies(side):
        return [
            pltpu.make_async_copy(total.at[index], ref, out_sem.at[index])
            for index, ref in ((0, image_grad_ref), (1, text_grad_ref))
        ]

    def finish(side):
        for start in range(0, rows, band):
            at = pl.ds(start, band)
            total[side, at, :] = scale * (
                total[side, at, :] - 2.0 * held[side, at, :].astype(jnp.float32)
            )
        for index, copy in enumerate(out_copies(side)):
            @pl.when(side == index)
            def _():
                copy.start()

    finish(side_b)
    receive(BOTH, side_a, pieces - 1)
    add_piece(BOTH, side_a, pieces - 1)
    finish(side_a)

    for kind in (NEAR, FAR, BOTH):
        for side in (side_a, side_b):
            stat_copy(kind, side).wait_send()

            def sent(c):
                block_copy(kind, side, c).wait_send()

            for_pieces(sent)
    for copy in out_copies(0):
        copy.wait()


def local(image_embeds, text_embeds, image_lse, text_lse, logit_scale):
    rows, width = image_embeds.shape
    piece = 128
    pieces = rows // piece
    dma = pltpu.SemaphoreType.DMA
    grad = jax.ShapeDtypeStruct((rows, width), jnp.float32)
    anywhere = pl.BlockSpec(memory_space=pl.ANY)
    return pl.pallas_call(
        functools.partial(kernel, piece),
        out_shape=(grad, grad),
        in_specs=[pl.BlockSpec(memory_space=pltpu.SMEM)] + [anywhere] * 4,
        out_specs=(anywhere, anywhere),
        scratch_shapes=[
            pltpu.VMEM((2, rows, width), jnp.bfloat16),
            pltpu.VMEM((2, 1, rows), jnp.float32),
            pltpu.VMEM((2, rows, LANES), jnp.float32),
            pltpu.VMEM((3, 2, rows, width), jnp.bfloat16),
            pltpu.VMEM((3, 2, 1, rows), jnp.float32),
            pltpu.VMEM((2, rows, width), jnp.float32),
            dma((4,)),
            dma((3, 2, pieces)),
            dma((3, 2, pieces)),
            dma((3, 2)),
            dma((3, 2)),
            dma((2,)),
        ],
        compiler_params=pltpu.CompilerParams(
            collective_id=0, has_side_effects=True, vmem_limit_bytes=32 * 1024 * 1024
        ),
        cost_estimate=pl.CostEstimate(
            flops=32 * rows * rows * width,
            bytes_accessed=12 * rows * width,
            transcendentals=16 * rows * rows,
        ),
    )(
        logit_scale.reshape(1, 1),
        image_embeds,
        text_embeds,
        image_lse.reshape(1, rows),
        text_lse.reshape(1, rows),
    )


def solution(mesh):
    return jax.shard_map(
        local,
        mesh=mesh,
        in_specs=(
            P(("outer", "inner"), None),
            P(("outer", "inner"), None),
            P(("outer", "inner")),
            P(("outer", "inner")),
            P(),
        ),
        out_specs=(P(("outer", "inner"), None), P(("outer", "inner"), None)),
        check_vma=False,
    )
```

time: 87.2 us -> 45.7 us (0.52)
  waiting for transfers between devices: 63.9 us -> 0 us
  Pallas kernels: 0 us -> 39.5 us
  starting transfers between devices: 10.9 us -> 0 us
  matrix products: 9.32 us -> 0 us
  local copies, waits for them, and re-layouts: 0.71 us -> 4.71 us
    ppermute x9 -> x0, waiting for transfers between devices: 63.9 us -> none  [shifted(): return lax.ppermute(value, axis, pairs)]
    pallas_call x0 -> x1, Pallas kernels: none -> 39.5 us  [local(): pl.pallas_call(functools.partial(kernel, piece), out_shape=(grad, grad),...]
    ppermute x9 -> x0, starting transfers between devices: 10.9 us -> none  [shifted(): return lax.ppermute(value, axis, pairs)]
    dot_general x12 -> x0, matrix products: 9.32 us -> none  [the longest x4 3.74 us: tile_weights(): lax.dot_general(images, text_rows, (((1,), (1,)), ((), ())), preferred_el...]
    unnamed x8 -> x10, local copies, waits for them, and re-layouts: 0.69 us -> 4.71 us
  transfers between devices with their start and end apart: 9 -> 0, of which waited for: 4 -> 0; matrix products, arithmetic and copies ran while one was open for 10% -> 0% of each run, Pallas kernels for 0% -> 0%
where the time goes in v1:
time: 45.7 us; the launch traced here: 45.5 us
  Pallas kernels  39.5 us (86%)
  local copies, waits for them, and re-layouts  4.71 us (10%)
  between operations  1.3 us (3%)
    pallas_call x1, Pallas kernels, local(): pl.pallas_call(functools.partial(kernel, piece), out_shape=(grad, grad),...  39.5 us
    unnamed x10, local copies, waits for them, and re-layouts  4.71 us

profile of v1, /device:TPU:0, one launch (start us, length us, event | category | flops | bytes accessed | tf_op | source)
XLA Modules:
  0.0 45.5 jit_solution(9658658357079665006)
XLA Ops:
  1.3 0.0 copy-start.3
  1.3 0.0 copy-start.2
  1.3 0.7 %copy-done.3 = f32[512]{0:T(512)S(1)} copy-done((f32[512]{0:T(512)S(1)}, f32[512]{0:T(512)}, u32[]{:S(2)}) %copy-start.3) | copy-done | bytes 2072
  2.0 0.0 copy-done.2
  2.0 0.0 copy-start
  2.0 1.0 %copy-done = bf16[512,512]{1,0:T(8,128)(2,1)S(1)} copy-done((bf16[512,512]{1,0:T(8,128)(2,1)S(1)}, bf16[512,512]{1,0:T(8,128)(2,1)}, u32[]{:S(2)}) %copy-start) | copy-done | bytes 524312
  3.0 0.0 copy-start.1
  3.0 1.0 %copy-done.1 = bf16[512,512]{1,0:T(8,128)(2,1)S(1)} copy-done((bf16[512,512]{1,0:T(8,128)(2,1)S(1)}, bf16[512,512]{1,0:T(8,128)(2,1)}, u32[]{:S(2)}) %copy-start.1) | copy-done | bytes 524312
  4.1 39.5 %shard_map.68 = (f32[512,512]{1,0:T(8,128)S(1)}, f32[512,512]{1,0:T(8,128)S(1)}) custom-call(f32[1,1]{1,0:T(1,128)} %bitcast.3.scale_ref, bf16[512,512]{1,0:T(8,128)(2,1)S(1)} %copy-done, bf16[512,512]{1,0:T(8,128)(2,1)S(1)} %copy-done.1, f32[1,512]{1,0:T(1,128)S(1)} %bitcast.4, f32[1,512]{1,0:T(1,128)S(1)} %bitcast.5), custom_call_target="tpu_custom_call" | custom-call | flops 4294967296 | bytes 3145728 | tf_op jit(solution)/shard_map/pallas_call | solution.py:245
  43.5 1.0 %copy.10 = f32[512,512]{1,0:T(8,128)} copy(f32[512,512]{1,0:T(8,128)S(1)} %get-tuple-element.4) | data formatting | bytes 2097152
  44.5 1.0 %copy.11 = f32[512,512]{1,0:T(8,128)} copy(f32[512,512]{1,0:T(8,128)S(1)} %get-tuple-element.5) | data formatting | bytes 2097152
Async XLA Ops:
  1.3 0.7 %copy-start.3 = (f32[512]{0:T(512)S(1)}, f32[512]{0:T(512)}, u32[]{:S(2)}) copy-start(f32[512]{0:T(512)} %param.8) | copy-start | bytes 6148
  1.3 0.7 %copy-start.2 = (f32[512]{0:T(512)S(1)}, f32[512]{0:T(512)}, u32[]{:S(2)}) copy-start(f32[512]{0:T(512)} %param.7) | copy-start | bytes 6148
  2.0 1.0 %copy-start = (bf16[512,512]{1,0:T(8,128)(2,1)S(1)}, bf16[512,512]{1,0:T(8,128)(2,1)}, u32[]{:S(2)}) copy-start(bf16[512,512]{1,0:T(8,128)(2,1)} %images_ref.1) | copy-start | bytes 1572868
  3.0 1.0 %copy-start.1 = (bf16[512,512]{1,0:T(8,128)(2,1)S(1)}, bf16[512,512]{1,0:T(8,128)(2,1)}, u32[]{:S(2)}) copy-start(bf16[512,512]{1,0:T(8,128)(2,1)} %texts_ref.1) | copy-start | bytes 1572868

commit v2 on v1

--- a/solution.py
+++ b/solution.py
@@ -22,22 +22,20 @@
     texts_ref,
     image_lse_ref,
     text_lse_ref,
-    image_grad_ref,
-    text_grad_ref,
+    total,
     held,
     stat,
     column,
     got,
     got_stat,
-    total,
     load_sem,
     send_sem,
     recv_sem,
     stat_send_sem,
     stat_recv_sem,
-    out_sem,
 ):
     rows, width = images_ref.shape
+    band = 256
     pieces = rows // piece
     outer, inner = lax.axis_index("outer"), lax.axis_index("inner")
     n_outer, n_inner = lax.axis_size("outer"), lax.axis_size("inner")
@@ -124,115 +122,97 @@
     def send_near(c):
         block_copy(NEAR, side_b, c).start()
 
-    def send_far(c):
-        block_copy(FAR, side_b, c).start()
-
     for_pieces(send_first)
     for_pieces(send_near)
-    for_pieces(send_far)
 
     for side in (0, 1):
         column[side] = jnp.broadcast_to(stat[side] * LOG2E, (LANES, rows)).T
-
-    def contribution(side, start, size, block, row):
+    total[side_b] = jnp.zeros((rows, width), jnp.float32)
+
+    def contribution(side, start, block, row):
         scores = factor * lax.dot_general(
-            held[1 - side, pl.ds(start, size), :], block, NT,
+            held[1 - side, pl.ds(start, band), :], block, NT,
             preferred_element_type=jnp.float32,
         )
         wide = jnp.concatenate(
-            [column[1 - side, pl.ds(start, size), :]] * (block.shape[0] // LANES), axis=1
+            [column[1 - side, pl.ds(start, band), :]] * (block.shape[0] // LANES), axis=1
         )
         weights = (jnp.exp2(scores - wide) + jnp.exp2(scores - row)).astype(jnp.bfloat16)
         return jnp.dot(weights, block, preferred_element_type=jnp.float32)
 
-    band = 256
-
-    def add_piece(kind, side, c):
-        block = got[kind, side, span(c), :]
-        row = got_stat[kind, side, :, span(c)] * LOG2E
+    def own(side, at):
+        return held[side, at, :], stat[side, :, at]
+
+    def arrived(kind, side, at):
+        return got[kind, side, at, :], got_stat[kind, side, :, at]
+
+    def add(side, parts, fresh=False):
+        block = jnp.concatenate([part[0] for part in parts], axis=0)
+        row = jnp.concatenate([part[1] for part in parts], axis=1) * LOG2E
         for start in range(0, rows, band):
-            total[side, pl.ds(start, band), :] += contribution(side, start, band, block, row)
-
-    for side in (0, 1):
-        block = held[side]
-        row = stat[side] * LOG2E
-        for start in range(0, rows, band):
-            total[side, pl.ds(start, band), :] = contribution(side, start, band, block, row)
+            term = contribution(side, start, block, row)
+            if fresh:
+                total[side, pl.ds(start, band), :] = term
+            else:
+                total[side, pl.ds(start, band), :] += term
 
     def receive(kind, side, c):
         block_copy(kind, side, c).wait_recv()
 
-    stat_copy(NEAR, side_a).wait_recv()
-
-    def near_a(c):
-        receive(NEAR, side_a, c)
-        add_piece(NEAR, side_a, c)
-
-    for_pieces(near_a)
+    half = rows // 2
+    for index in range(2):
+        add(side_a, [own(side_a, pl.ds(index * half, half))], fresh=index == 0)
 
     for side in (side_a, side_b):
+        stat_copy(NEAR, side).wait_recv()
         stat_copy(FAR, side).wait_recv()
         stat_copy(BOTH, side).start()
-    stat_copy(NEAR, side_b).wait_recv()
 
     def early(c):
+        at = span(c)
         receive(FAR, side_a, c)
         block_copy(BOTH, side_a, c).start()
-        add_piece(FAR, side_a, c)
+        block_copy(FAR, side_a, c).wait_send()
+        block_copy(FAR, side_b, c).start()
+        receive(NEAR, side_a, c)
+        add(side_a, [arrived(FAR, side_a, at), arrived(NEAR, side_a, at)])
         receive(NEAR, side_b, c)
-        add_piece(NEAR, side_b, c)
+        add(side_b, [own(side_b, at), arrived(NEAR, side_b, at)])
 
     for_pieces(early)
 
     for side in (side_a, side_b):
         stat_copy(BOTH, side).wait_recv()
 
+    def last(index):
+        for c in range(index * pieces // 2, (index + 1) * pieces // 2):
+            receive(BOTH, side_a, c)
+        add(side_a, [arrived(BOTH, side_a, pl.ds(index * half, half))])
+
     def late(c):
+        at = span(c)
         receive(FAR, side_b, c)
         block_copy(BOTH, side_b, c).start()
-        add_piece(FAR, side_b, c)
         receive(BOTH, side_b, c)
-        add_piece(BOTH, side_b, c)
-
-        @pl.when(c > 0)
+        add(side_b, [arrived(FAR, side_b, at), arrived(BOTH, side_b, at)])
+
+        @pl.when(c == pieces // 2)
         def _():
-            receive(BOTH, side_a, c - 1)
-            add_piece(BOTH, side_a, c - 1)
+            last(0)
 
     for_pieces(late)
-
-    def out_copies(side):
-        return [
-            pltpu.make_async_copy(total.at[index], ref, out_sem.at[index])
-            for index, ref in ((0, image_grad_ref), (1, text_grad_ref))
-        ]
-
-    def finish(side):
-        for start in range(0, rows, band):
-            at = pl.ds(start, band)
-            total[side, at, :] = scale * (
-                total[side, at, :] - 2.0 * held[side, at, :].astype(jnp.float32)
-            )
-        for index, copy in enumerate(out_copies(side)):
-            @pl.when(side == index)
-            def _():
-                copy.start()
-
-    finish(side_b)
-    receive(BOTH, side_a, pieces - 1)
-    add_piece(BOTH, side_a, pieces - 1)
-    finish(side_a)
+    last(1)
 
     for kind in (NEAR, FAR, BOTH):
         for side in (side_a, side_b):
             stat_copy(kind, side).wait_send()
+            if kind == FAR and side is side_a:
+                continue
 
             def sent(c):
                 block_copy(kind, side, c).wait_send()
 
             for_pieces(sent)
-    for copy in out_copies(0):
-        copy.wait()
 
 
 def local(image_embeds, text_embeds, image_lse, text_lse, logit_scale):
@@ -240,29 +220,26 @@
     piece = 128
     pieces = rows // piece
     dma = pltpu.SemaphoreType.DMA
-    grad = jax.ShapeDtypeStruct((rows, width), jnp.float32)
-    anywhere = pl.BlockSpec(memory_space=pl.ANY)
-    return pl.pallas_call(
+    anywhere = pl.BlockSpec(memory_space=pltpu.HBM)
+    total = pl.pallas_call(
         functools.partial(kernel, piece),
-        out_shape=(grad, grad),
+        out_shape=jax.ShapeDtypeStruct((2, rows, width), jnp.float32),
         in_specs=[pl.BlockSpec(memory_space=pltpu.SMEM)] + [anywhere] * 4,
-        out_specs=(anywhere, anywhere),
+        out_specs=pl.BlockSpec(memory_space=pltpu.VMEM),
         scratch_shapes=[
             pltpu.VMEM((2, rows, width), jnp.bfloat16),
             pltpu.VMEM((2, 1, rows), jnp.float32),
             pltpu.VMEM((2, rows, LANES), jnp.float32),
             pltpu.VMEM((3, 2, rows, width), jnp.bfloat16),
             pltpu.VMEM((3, 2, 1, rows), jnp.float32),
-            pltpu.VMEM((2, rows, width), jnp.float32),
             dma((4,)),
             dma((3, 2, pieces)),
             dma((3, 2, pieces)),
             dma((3, 2)),
             dma((3, 2)),
-            dma((2,)),
         ],
         compiler_params=pltpu.CompilerParams(
-            collective_id=0, has_side_effects=True, vmem_limit_bytes=32 * 1024 * 1024
+            collective_id=0, has_side_effects=True, vmem_limit_bytes=60 * 1024 * 1024
         ),
         cost_estimate=pl.CostEstimate(
             flops=32 * rows * rows * width,
@@ -276,6 +253,9 @@
         image_lse.reshape(1, rows),
         text_lse.reshape(1, rows),
     )
+    image_grad = logit_scale * (total[0] - 2.0 * text_embeds.astype(jnp.float32))
+    text_grad = logit_scale * (total[1] - 2.0 * image_embeds.astype(jnp.float32))
+    return image_grad, text_grad
 
 
 def solution(mesh):

time: 45.7 us -> 42.1 us (0.921)
  local copies, waits for them, and re-layouts: 4.71 us -> 0.01 us
  other arithmetic: 0 us -> 3.22 us
  Pallas kernels: 39.5 us -> 37.4 us
    unnamed x10 -> x4, local copies, waits for them, and re-layouts: 4.71 us -> 0.01 us
    mul x0 -> x1, other arithmetic: none -> 3.22 us  [local(): logit_scale * (total[1] - 2.0 * image_embeds.astype(jnp.float32))]
    pallas_call x1, Pallas kernels: 39.5 us -> 37.4 us  [local(): pl.pallas_call(functools.partial(kernel, piece), out_shape=jax.ShapeDtype...]
where the time goes in v2:
time: 42.1 us; the launch traced here: 41.9 us
  Pallas kernels  37.4 us (89%)
  other arithmetic  3.22 us (8%)
  between operations  1.32 us (3%)
    pallas_call x1, Pallas kernels, local(): pl.pallas_call(functools.partial(kernel, piece), out_shape=jax.ShapeDtype...  37.4 us
    mul x1, other arithmetic, local(): logit_scale * (total[1] - 2.0 * image_embeds.astype(jnp.float32))  3.22 us

profile of v2, /device:TPU:0, one launch (start us, length us, event | category | flops | bytes accessed | tf_op | source)
XLA Modules:
  0.0 41.9 jit_solution(18006912340918753788)
XLA Ops:
  1.3 0.0 copy-start
  1.3 0.0 copy-start.1
  1.3 37.4 %shard_map.68 = f32[2,512,512]{2,1,0:T(8,128)} custom-call(f32[1,1]{1,0:T(1,128)} %bitcast.11.scale_ref, bf16[512,512]{1,0:T(8,128)(2,1)} %images_ref.1, bf16[512,512]{1,0:T(8,128)(2,1)} %texts_ref.1, f32[1,512]{1,0:T(1,128)} %bitcast.12, f32[1,512]{1,0:T(1,128)} %bitcast.13), custom_call_target="tpu_custom_call" | custom-call | flops 4294967296 | bytes 3145728 | tf_op jit(solution)/shard_map/pallas_call | solution.py:224
  38.7 0.0 copy-done
  38.7 0.0 copy-done.1
  38.7 3.2 %fusion = (f32[512,512]{1,0:T(8,128)}, f32[512,512]{1,0:T(8,128)}) fusion(bf16[512,512]{1,0:T(8,128)(2,1)S(1)} %copy-done, f32[2,512,512]{2,1,0:T(8,128)} %shard_map.68, f32[]{:T(128)} %copy.7, bf16[512,512]{1,0:T(8,128)(2,1)S(1)} %copy-done.1), kind=kLoop, calls=%fused_computation.1 | loop fusion | flops 2097152 | bytes 5242884 | tf_op jit(solution)/shard_map/mul | solution.py:257
Async XLA Ops:
  1.3 37.4 %copy-start = (bf16[512,512]{1,0:T(8,128)(2,1)S(1)}, bf16[512,512]{1,0:T(8,128)(2,1)}, u32[]{:S(2)}) copy-start(bf16[512,512]{1,0:T(8,128)(2,1)} %images_ref.1) | copy-start | bytes 1572868
  1.3 37.4 %copy-start.1 = (bf16[512,512]{1,0:T(8,128)(2,1)S(1)}, bf16[512,512]{1,0:T(8,128)(2,1)}, u32[]{:S(2)}) copy-start(bf16[512,512]{1,0:T(8,128)(2,1)} %texts_ref.1) | copy-start | bytes 1572868

commit v3 on v2

--- a/solution.py
+++ b/solution.py
@@ -170,10 +170,10 @@
 
     def early(c):
         at = span(c)
+        block_copy(FAR, side_a, c).wait_send()
+        block_copy(FAR, side_b, c).start()
         receive(FAR, side_a, c)
         block_copy(BOTH, side_a, c).start()
-        block_copy(FAR, side_a, c).wait_send()
-        block_copy(FAR, side_b, c).start()
         receive(NEAR, side_a, c)
         add(side_a, [arrived(FAR, side_a, at), arrived(NEAR, side_a, at)])
         receive(NEAR, side_b, c)

time: 42.1 us -> 41.9 us (level)
  no operation moved by 1% of the time
where the time goes in v3:
time: 41.9 us; the launch traced here: 41.7 us
  Pallas kernels  37.2 us (89%)
  other arithmetic  3.22 us (8%)
  between operations  1.32 us (3%)
    pallas_call x1, Pallas kernels, local(): pl.pallas_call(functools.partial(kernel, piece), out_shape=jax.ShapeDtype...  37.2 us
    mul x1, other arithmetic, local(): logit_scale * (total[1] - 2.0 * image_embeds.astype(jnp.float32))  3.22 us

profile of v3, /device:TPU:0, one launch (start us, length us, event | category | flops | bytes accessed | tf_op | source)
XLA Modules:
  0.0 41.7 jit_solution(3808810816783866432)
XLA Ops:
  1.3 0.0 copy-start
  1.3 0.0 copy-start.1
  1.3 37.2 %shard_map.68 = f32[2,512,512]{2,1,0:T(8,128)} custom-call(f32[1,1]{1,0:T(1,128)} %bitcast.11.scale_ref, bf16[512,512]{1,0:T(8,128)(2,1)} %images_ref.1, bf16[512,512]{1,0:T(8,128)(2,1)} %texts_ref.1, f32[1,512]{1,0:T(1,128)} %bitcast.12, f32[1,512]{1,0:T(1,128)} %bitcast.13), custom_call_target="tpu_custom_call" | custom-call | flops 4294967296 | bytes 3145728 | tf_op jit(solution)/shard_map/pallas_call | solution.py:224
  38.5 0.0 copy-done
  38.5 0.0 copy-done.1
  38.5 3.2 %fusion = (f32[512,512]{1,0:T(8,128)}, f32[512,512]{1,0:T(8,128)}) fusion(bf16[512,512]{1,0:T(8,128)(2,1)S(1)} %copy-done, f32[2,512,512]{2,1,0:T(8,128)} %shard_map.68, f32[]{:T(128)} %copy.7, bf16[512,512]{1,0:T(8,128)(2,1)S(1)} %copy-done.1), kind=kLoop, calls=%fused_computation.1 | loop fusion | flops 2097152 | bytes 5242884 | tf_op jit(solution)/shard_map/mul | solution.py:257
Async XLA Ops:
  1.3 37.2 %copy-start = (bf16[512,512]{1,0:T(8,128)(2,1)S(1)}, bf16[512,512]{1,0:T(8,128)(2,1)}, u32[]{:S(2)}) copy-start(bf16[512,512]{1,0:T(8,128)(2,1)} %images_ref.1) | copy-start | bytes 1572868
  1.3 37.2 %copy-start.1 = (bf16[512,512]{1,0:T(8,128)(2,1)S(1)}, bf16[512,512]{1,0:T(8,128)(2,1)}, u32[]{:S(2)}) copy-start(bf16[512,512]{1,0:T(8,128)(2,1)} %texts_ref.1) | copy-start | bytes 1572868

commit v4 on v3

--- a/solution.py
+++ b/solution.py
@@ -115,14 +115,18 @@
         for kind in (FAR, NEAR):
             stat_copy(kind, side).start()
 
-    def send_first(c):
-        block_copy(FAR, side_a, c).start()
-        block_copy(NEAR, side_a, c).start()
+    ahead = 2
+
+    def send_far(m):
+        late_side = m // pieces
+        block_copy(FAR, side_a + late_side * (side_b - side_a), m % pieces).start()
 
     def send_near(c):
         block_copy(NEAR, side_b, c).start()
 
-    for_pieces(send_first)
+    for c in range(ahead):
+        send_far(c)
+        block_copy(NEAR, side_a, c).start()
     for_pieces(send_near)
 
     for side in (0, 1):
@@ -171,9 +175,18 @@
     def early(c):
         at = span(c)
         block_copy(FAR, side_a, c).wait_send()
-        block_copy(FAR, side_b, c).start()
+        send_far(c + ahead)
         receive(FAR, side_a, c)
-        block_copy(BOTH, side_a, c).start()
+        block_copy(NEAR, side_a, c).wait_send()
+
+        @pl.when(c < pieces - ahead)
+        def _():
+            block_copy(NEAR, side_a, c + ahead).start()
+
+        @pl.when(c >= pieces - ahead)
+        def _():
+            block_copy(BOTH, side_a, c + ahead - pieces).start()
+
         receive(NEAR, side_a, c)
         add(side_a, [arrived(FAR, side_a, at), arrived(NEAR, side_a, at)])
         receive(NEAR, side_b, c)
@@ -191,6 +204,14 @@
 
     def late(c):
         at = span(c)
+        block_copy(FAR, side_b, c).wait_send()
+        block_copy(BOTH, side_a, c).wait_send()
+
+        @pl.when(c < pieces - ahead)
+        def _():
+            send_far(c + ahead + pieces)
+            block_copy(BOTH, side_a, c + ahead).start()
+
         receive(FAR, side_b, c)
         block_copy(BOTH, side_b, c).start()
         receive(BOTH, side_b, c)
@@ -206,13 +227,12 @@
     for kind in (NEAR, FAR, BOTH):
         for side in (side_a, side_b):
             stat_copy(kind, side).wait_send()
-            if kind == FAR and side is side_a:
-                continue
-
-            def sent(c):
-                block_copy(kind, side, c).wait_send()
-
-            for_pieces(sent)
+    for kind in (NEAR, BOTH):
+
+        def sent(c):
+            block_copy(kind, side_b, c).wait_send()
+
+        for_pieces(sent)
 
 
 def local(image_embeds, text_embeds, image_lse, text_lse, logit_scale):
@@ -223,7 +243,7 @@
     anywhere = pl.BlockSpec(memory_space=pltpu.HBM)
     total = pl.pallas_call(
         functools.partial(kernel, piece),
-        out_shape=jax.ShapeDtypeStruct((2, rows, width), jnp.float32),
+        out_shape=pltpu.VMEM((2, rows, width), jnp.float32),
         in_specs=[pl.BlockSpec(memory_space=pltpu.SMEM)] + [anywhere] * 4,
         out_specs=pl.BlockSpec(memory_space=pltpu.VMEM),
         scratch_shapes=[

time: 41.9 us -> 38.1 us (0.909)
  Pallas kernels: 37.2 us -> 34.9 us
  other arithmetic: 3.22 us -> 1.68 us
    pallas_call x1, Pallas kernels: 37.2 us -> 34.9 us  [local(): pl.pallas_call(functools.partial(kernel, piece), out_shape=pltpu.VMEM((2,...]
    mul x1, other arithmetic: 3.22 us -> 1.68 us  [local(): logit_scale * (total[1] - 2.0 * image_embeds.astype(jnp.float32))]
where the time goes in v4:
time: 38.1 us; the launch traced here: 37.9 us
  Pallas kernels  34.9 us (92%)
  other arithmetic  1.68 us (4%)
  between operations  1.32 us (3%)
    pallas_call x1, Pallas kernels, local(): pl.pallas_call(functools.partial(kernel, piece), out_shape=pltpu.VMEM((2,...  34.9 us
    mul x1, other arithmetic, local(): logit_scale * (total[1] - 2.0 * image_embeds.astype(jnp.float32))  1.68 us

profile of v4, /device:TPU:0, one launch (start us, length us, event | category | flops | bytes accessed | tf_op | source)
XLA Modules:
  0.0 37.9 jit_solution(15225599903842684073)
XLA Ops:
  1.3 0.0 copy-start
  1.3 0.0 copy-start.1
  1.3 34.9 %shard_map.68 = f32[2,512,512]{2,1,0:T(8,128)S(1)} custom-call(f32[1,1]{1,0:T(1,128)} %bitcast.11.scale_ref, bf16[512,512]{1,0:T(8,128)(2,1)} %images_ref.1, bf16[512,512]{1,0:T(8,128)(2,1)} %texts_ref.1, f32[1,512]{1,0:T(1,128)} %bitcast.12, f32[1,512]{1,0:T(1,128)} %bitcast.13), custom_call_target="tpu_custom_call" | custom-call | flops 4294967296 | bytes 3145728 | tf_op jit(solution)/shard_map/pallas_call | solution.py:244
  36.2 0.0 copy-done
  36.2 0.0 copy-done.1
  36.2 1.7 %fusion = (f32[512,512]{1,0:T(8,128)}, f32[512,512]{1,0:T(8,128)}) fusion(bf16[512,512]{1,0:T(8,128)(2,1)S(1)} %copy-done, f32[2,512,512]{2,1,0:T(8,128)S(1)} %shard_map.68, f32[]{:T(128)} %copy.7, bf16[512,512]{1,0:T(8,128)(2,1)S(1)} %copy-done.1), kind=kLoop, calls=%fused_computation.1 | loop fusion | flops 2097152 | bytes 5242884 | tf_op jit(solution)/shard_map/mul | solution.py:277
Async XLA Ops:
  1.3 34.9 %copy-start = (bf16[512,512]{1,0:T(8,128)(2,1)S(1)}, bf16[512,512]{1,0:T(8,128)(2,1)}, u32[]{:S(2)}) copy-start(bf16[512,512]{1,0:T(8,128)(2,1)} %images_ref.1) | copy-start | bytes 1572868
  1.3 34.9 %copy-start.1 = (bf16[512,512]{1,0:T(8,128)(2,1)S(1)}, bf16[512,512]{1,0:T(8,128)(2,1)}, u32[]{:S(2)}) copy-start(bf16[512,512]{1,0:T(8,128)(2,1)} %texts_ref.1) | copy-start | bytes 1572868

commit v5 on v4

--- a/solution.py
+++ b/solution.py
@@ -33,6 +33,7 @@
     recv_sem,
     stat_send_sem,
     stat_recv_sem,
+    ready_sem,
 ):
     rows, width = images_ref.shape
     band = 256
@@ -56,22 +57,45 @@
     for load in loads:
         load.start()
 
+    first, last_group = outer == 0, outer == n_outer - 1
     barrier = pltpu.get_barrier_semaphore()
     for step in (1, -1):
         pl.semaphore_signal(
-            barrier, inc=1, device_id={"outer": (outer + step + n_outer) % n_outer},
-            device_id_type=MESH,
-        )
-        pl.semaphore_signal(
             barrier, inc=1, device_id={"inner": (inner + step + n_inner) % n_inner},
             device_id_type=MESH,
         )
-    pl.semaphore_wait(barrier, 4)
+    pl.semaphore_signal(
+        barrier, inc=1, device_id={"outer": (outer - 1 + n_outer) % n_outer},
+        device_id_type=MESH,
+    )
+
+    @pl.when(jnp.logical_not(last_group))
+    def _():
+        pl.semaphore_signal(
+            barrier, inc=1, device_id={"outer": (outer + 1) % n_outer}, device_id_type=MESH
+        )
+
+    @pl.when(first)
+    def _():
+        pl.semaphore_wait(barrier, 3)
+
+    @pl.when(jnp.logical_not(first))
+    def _():
+        pl.semaphore_wait(barrier, 4)
+
+    @pl.when(last_group)
+    def _():
+        pl.semaphore_signal(
+            ready_sem, inc=1, device_id={"outer": (outer + 1) % n_outer}, device_id_type=MESH
+        )
+
     for load in loads:
         load.wait()
 
     side_a = 1 - inner % 2
     side_b = inner % 2
+    wait_soon = jnp.logical_and(first, side_a == 1)
+    wait_later = jnp.logical_and(first, side_a == 0)
 
     def target(kind, side):
         step = 1 - 2 * side
@@ -111,9 +135,9 @@
 
         lax.fori_loop(0, pieces, step, 0)
 
-    for side in (side_a, side_b):
-        for kind in (FAR, NEAR):
-            stat_copy(kind, side).start()
+    stat_copy(FAR, 0).start()
+    for side in (0, 1):
+        stat_copy(NEAR, side).start()
 
     ahead = 2
 
@@ -124,8 +148,12 @@
     def send_near(c):
         block_copy(NEAR, side_b, c).start()
 
+    def open_far():
+        for c in range(ahead):
+            send_far(c)
+
+    pl.when(jnp.logical_not(wait_soon))(open_far)
     for c in range(ahead):
-        send_far(c)
         block_copy(NEAR, side_a, c).start()
     for_pieces(send_near)
 
@@ -167,14 +195,29 @@
     for index in range(2):
         add(side_a, [own(side_a, pl.ds(index * half, half))], fresh=index == 0)
 
+    @pl.when(wait_soon)
+    def _():
+        pl.semaphore_wait(ready_sem, 1)
+        open_far()
+
+    @pl.when(jnp.logical_not(wait_later))
+    def _():
+        stat_copy(FAR, 1).start()
+
     for side in (side_a, side_b):
         stat_copy(NEAR, side).wait_recv()
-        stat_copy(FAR, side).wait_recv()
-        stat_copy(BOTH, side).start()
+    stat_copy(FAR, side_a).wait_recv()
+    stat_copy(BOTH, side_a).start()
 
     def early(c):
         at = span(c)
         block_copy(FAR, side_a, c).wait_send()
+
+        @pl.when(jnp.logical_and(wait_later, c == pieces - ahead))
+        def _():
+            pl.semaphore_wait(ready_sem, 1)
+            stat_copy(FAR, 1).start()
+
         send_far(c + ahead)
         receive(FAR, side_a, c)
         block_copy(NEAR, side_a, c).wait_send()
@@ -194,13 +237,7 @@
 
     for_pieces(early)
 
-    for side in (side_a, side_b):
-        stat_copy(BOTH, side).wait_recv()
-
-    def last(index):
-        for c in range(index * pieces // 2, (index + 1) * pieces // 2):
-            receive(BOTH, side_a, c)
-        add(side_a, [arrived(BOTH, side_a, pl.ds(index * half, half))])
+    stat_copy(BOTH, side_b).wait_recv()
 
     def late(c):
         at = span(c)
@@ -214,15 +251,30 @@
 
         receive(FAR, side_b, c)
         block_copy(BOTH, side_b, c).start()
+
+        @pl.when(c == 0)
+        def _():
+            stat_copy(FAR, side_b).wait_recv()
+            stat_copy(BOTH, side_b).start()
+
         receive(BOTH, side_b, c)
         add(side_b, [arrived(FAR, side_b, at), arrived(BOTH, side_b, at)])
 
         @pl.when(c == pieces // 2)
         def _():
-            last(0)
+            stat_copy(BOTH, side_a).wait_recv()
+            for index in range(pieces // 2):
+                receive(BOTH, side_a, index)
+            add(side_a, [arrived(BOTH, side_a, pl.ds(0, half))])
+
+        @pl.when(c > pieces // 2)
+        def _():
+            receive(BOTH, side_a, c - 1)
+            add(side_a, [arrived(BOTH, side_a, span(c - 1))])
 
     for_pieces(late)
-    last(1)
+    receive(BOTH, side_a, pieces - 1)
+    add(side_a, [arrived(BOTH, side_a, span(pieces - 1))])
 
     for kind in (NEAR, FAR, BOTH):
         for side in (side_a, side_b):
@@ -257,6 +309,7 @@
             dma((3, 2, pieces)),
             dma((3, 2)),
             dma((3, 2)),
+            pltpu.SemaphoreType.REGULAR,
         ],
         compiler_params=pltpu.CompilerParams(
             collective_id=0, has_side_effects=True, vmem_limit_bytes=60 * 1024 * 1024

time: 38.1 us -> 37.9 us (level)
  no operation moved by 1% of the time
where the time goes in v5:
time: 37.9 us; the launch traced here: 37.7 us
  Pallas kernels  34.7 us (92%)
  other arithmetic  1.68 us (4%)
  between operations  1.32 us (3%)
    pallas_call x1, Pallas kernels, local(): pl.pallas_call(functools.partial(kernel, piece), out_shape=pltpu.VMEM((2,...  34.7 us
    mul x1, other arithmetic, local(): logit_scale * (total[1] - 2.0 * image_embeds.astype(jnp.float32))  1.68 us

profile of v5, /device:TPU:0, one launch (start us, length us, event | category | flops | bytes accessed | tf_op | source)
XLA Modules:
  0.0 37.7 jit_solution(11878070334181934982)
XLA Ops:
  1.3 0.0 copy-start
  1.3 0.0 copy-start.1
  1.3 34.7 %shard_map.68 = f32[2,512,512]{2,1,0:T(8,128)S(1)} custom-call(f32[1,1]{1,0:T(1,128)} %bitcast.11.scale_ref, bf16[512,512]{1,0:T(8,128)(2,1)} %images_ref.1, bf16[512,512]{1,0:T(8,128)(2,1)} %texts_ref.1, f32[1,512]{1,0:T(1,128)} %bitcast.12, f32[1,512]{1,0:T(1,128)} %bitcast.13), custom_call_target="tpu_custom_call" | custom-call | flops 4294967296 | bytes 3145728 | tf_op jit(solution)/shard_map/pallas_call | solution.py:296
  36.0 0.0 copy-done
  36.0 0.0 copy-done.1
  36.1 1.7 %fusion = (f32[512,512]{1,0:T(8,128)}, f32[512,512]{1,0:T(8,128)}) fusion(bf16[512,512]{1,0:T(8,128)(2,1)S(1)} %copy-done, f32[2,512,512]{2,1,0:T(8,128)S(1)} %shard_map.68, f32[]{:T(128)} %copy.7, bf16[512,512]{1,0:T(8,128)(2,1)S(1)} %copy-done.1), kind=kLoop, calls=%fused_computation.1 | loop fusion | flops 2097152 | bytes 5242884 | tf_op jit(solution)/shard_map/mul | solution.py:330
Async XLA Ops:
  1.3 34.8 %copy-start = (bf16[512,512]{1,0:T(8,128)(2,1)S(1)}, bf16[512,512]{1,0:T(8,128)(2,1)}, u32[]{:S(2)}) copy-start(bf16[512,512]{1,0:T(8,128)(2,1)} %images_ref.1) | copy-start | bytes 1572868
  1.3 34.8 %copy-start.1 = (bf16[512,512]{1,0:T(8,128)(2,1)S(1)}, bf16[512,512]{1,0:T(8,128)(2,1)}, u32[]{:S(2)}) copy-start(bf16[512,512]{1,0:T(8,128)(2,1)} %texts_ref.1) | copy-start | bytes 1572868

commit v6 on v5

--- a/solution.py
+++ b/solution.py
@@ -92,10 +92,7 @@
     for load in loads:
         load.wait()
 
-    side_a = 1 - inner % 2
-    side_b = inner % 2
-    wait_soon = jnp.logical_and(first, side_a == 1)
-    wait_later = jnp.logical_and(first, side_a == 0)
+    side_a, side_b = 0, 1
 
     def target(kind, side):
         step = 1 - 2 * side
@@ -152,7 +149,7 @@
         for c in range(ahead):
             send_far(c)
 
-    pl.when(jnp.logical_not(wait_soon))(open_far)
+    open_far()
     for c in range(ahead):
         block_copy(NEAR, side_a, c).start()
     for_pieces(send_near)
@@ -195,12 +192,7 @@
     for index in range(2):
         add(side_a, [own(side_a, pl.ds(index * half, half))], fresh=index == 0)
 
-    @pl.when(wait_soon)
-    def _():
-        pl.semaphore_wait(ready_sem, 1)
-        open_far()
-
-    @pl.when(jnp.logical_not(wait_later))
+    @pl.when(jnp.logical_not(first))
     def _():
         stat_copy(FAR, 1).start()
 
@@ -213,7 +205,7 @@
         at = span(c)
         block_copy(FAR, side_a, c).wait_send()
 
-        @pl.when(jnp.logical_and(wait_later, c == pieces - ahead))
+        @pl.when(jnp.logical_and(first, c == pieces - ahead))
         def _():
             pl.semaphore_wait(ready_sem, 1)
             stat_copy(FAR, 1).start()
@@ -237,7 +229,12 @@
 
     for_pieces(early)
 
-    stat_copy(BOTH, side_b).wait_recv()
+    stat_copy(BOTH, side_a).wait_recv()
+
+    def forwarded(index):
+        for c in range(index * pieces // 2, (index + 1) * pieces // 2):
+            receive(BOTH, side_a, c)
+        add(side_a, [arrived(BOTH, side_a, pl.ds(index * half, half))])
 
     def late(c):
         at = span(c)
@@ -249,6 +246,14 @@
             send_far(c + ahead + pieces)
             block_copy(BOTH, side_a, c + ahead).start()
 
+        @pl.when(c == pieces // 2)
+        def _():
+            forwarded(0)
+
+        @pl.when(c == pieces - 1)
+        def _():
+            forwarded(1)
+
         receive(FAR, side_b, c)
         block_copy(BOTH, side_b, c).start()
 
@@ -256,25 +261,23 @@
         def _():
             stat_copy(FAR, side_b).wait_recv()
             stat_copy(BOTH, side_b).start()
-
-        receive(BOTH, side_b, c)
-        add(side_b, [arrived(FAR, side_b, at), arrived(BOTH, side_b, at)])
-
-        @pl.when(c == pieces // 2)
-        def _():
-            stat_copy(BOTH, side_a).wait_recv()
-            for index in range(pieces // 2):
-                receive(BOTH, side_a, index)
-            add(side_a, [arrived(BOTH, side_a, pl.ds(0, half))])
-
-        @pl.when(c > pieces // 2)
-        def _():
-            receive(BOTH, side_a, c - 1)
-            add(side_a, [arrived(BOTH, side_a, span(c - 1))])
+            add(side_b, [arrived(FAR, side_b, at)])
+
+        @pl.when(c == 1)
+        def _():
+            stat_copy(BOTH, side_b).wait_recv()
+
+        @pl.when(c > 0)
+        def _():
+            receive(BOTH, side_b, c - 1)
+            add(
+                side_b,
+                [arrived(FAR, side_b, at), arrived(BOTH, side_b, span(c - 1))],
+            )
 
     for_pieces(late)
-    receive(BOTH, side_a, pieces - 1)
-    add(side_a, [arrived(BOTH, side_a, span(pieces - 1))])
+    receive(BOTH, side_b, pieces - 1)
+    add(side_b, [arrived(BOTH, side_b, span(pieces - 1))])
 
     for kind in (NEAR, FAR, BOTH):
         for side in (side_a, side_b):

time: 37.9 us -> 42.8 us (1.13)
  the two profiles are of different devices: /device:TPU:0 before, /device:TPU:19 now
where the time goes in v6:
time: 42.8 us; the launch traced here: 42.6 us
  Pallas kernels  39.6 us (93%)
  other arithmetic  1.68 us (4%)
  between operations  1.32 us (3%)
    pallas_call x1, Pallas kernels, local(): pl.pallas_call(functools.partial(kernel, piece), out_shape=pltpu.VMEM((2,...  39.6 us
    mul x1, other arithmetic, local(): logit_scale * (total[1] - 2.0 * image_embeds.astype(jnp.float32))  1.68 us

profile of v6, /device:TPU:19, one launch (start us, length us, event | category | flops | bytes accessed | tf_op | source)
XLA Modules:
  0.0 42.6 jit_solution(9969451049686254094)
XLA Ops:
  1.3 0.0 copy-start
  1.3 0.0 copy-start.1
  1.3 39.6 %shard_map.68 = f32[2,512,512]{2,1,0:T(8,128)S(1)} custom-call(f32[1,1]{1,0:T(1,128)} %bitcast.11.scale_ref, bf16[512,512]{1,0:T(8,128)(2,1)} %images_ref.1, bf16[512,512]{1,0:T(8,128)(2,1)} %texts_ref.1, f32[1,512]{1,0:T(1,128)} %bitcast.12, f32[1,512]{1,0:T(1,128)} %bitcast.13), custom_call_target="tpu_custom_call" | custom-call | flops 4294967296 | bytes 3145728 | tf_op jit(solution)/shard_map/pallas_call | solution.py:299
  40.9 0.0 copy-done
  40.9 0.0 copy-done.1
  40.9 1.7 %fusion = (f32[512,512]{1,0:T(8,128)}, f32[512,512]{1,0:T(8,128)}) fusion(bf16[512,512]{1,0:T(8,128)(2,1)S(1)} %copy-done, f32[2,512,512]{2,1,0:T(8,128)S(1)} %shard_map.68, f32[]{:T(128)} %copy.7, bf16[512,512]{1,0:T(8,128)(2,1)S(1)} %copy-done.1), kind=kLoop, calls=%fused_computation.1 | loop fusion | flops 2097152 | bytes 5242884 | tf_op jit(solution)/shard_map/mul | solution.py:333
Async XLA Ops:
  1.3 39.6 %copy-start = (bf16[512,512]{1,0:T(8,128)(2,1)S(1)}, bf16[512,512]{1,0:T(8,128)(2,1)}, u32[]{:S(2)}) copy-start(bf16[512,512]{1,0:T(8,128)(2,1)} %images_ref.1) | copy-start | bytes 1572868
  1.3 39.6 %copy-start.1 = (bf16[512,512]{1,0:T(8,128)(2,1)S(1)}, bf16[512,512]{1,0:T(8,128)(2,1)}, u32[]{:S(2)}) copy-start(bf16[512,512]{1,0:T(8,128)(2,1)} %texts_ref.1) | copy-start | bytes 1572868
